TPU v7x, 256 devices: a whole 4x4x8 slice. The times are simulated.
256 devices in a mesh: dp: 2 (over core), seq: 8 (over z), expert: 16 (over y, x).
Axes of the slice: x: 4, y: 4, z: 8, core: 2. Of those that a mesh axis runs over, the one named last changes fastest.
Arguments:
- tokens: bfloat16 [16, 2048, 2560], P(('dp', 'seq'), 'expert'), may hold values from -6 to 6
- text_states: bfloat16 [16, 128, 4096], P('dp', None, 'seq'), may hold values from -6 to 6
- text_lengths: int32 [16], P('dp'), may hold values from 64 to 128
- mod_weight: bfloat16 [4096, 5120], P('seq', 'expert'), may hold values from -1 to 1
- router_weight: bfloat16 [2560, 4], replicated, may hold values from -0.125 to 0.125
- gate_weight: bfloat16 [2560, 13824], P('dp', 'expert'), may hold values from -0.125 to 0.125
- up_weight: bfloat16 [2560, 13824], P('dp', 'expert'), may hold values from -0.125 to 0.125
- down_weight: bfloat16 [13824, 2560], P('expert', 'dp'), may hold values from -0.109375 to 0.109375
- expert_ids: int32 [16, 2048, 2], P(('dp', 'seq'), 'expert'), may hold values from 0 to 3, all different within a row; in each aligned block of 128 rows (0 to 127, 128 to 255, ..., all dimensions but the last counted through in order) at most 68 rows name the same one
- dropped: int32 [16, 2048, 2], P(('dp', 'seq'), 'expert'), may hold values 0 or 1
Outputs:
- mixed: bfloat16 [16, 2048, 2560], P(('dp', 'seq'), 'expert')
Inputs may be any that keep to these rules, and one draw needn't show every extreme that they name: `expert_ids`: each row names 2 different experts. In every aligned block of 128 patches (one image's patches on one device) no expert is named by more than 68 rows, and some block reaches 68.
All inputs are finite; a program needn't handle non-finite values. No bound on the sum of `dropped` on one device may be relied on, other than what follows from the above.
Results may differ from a plain program's by a relative error of at most 0.014.
Values may be sent and summed in bfloat16 or wider, within the bound.
No kernel may reach another device: no remote copies, remote signals or barrier semaphores. Data moves between devices by JAX's collectives and lax.ppermute only.
A program may use at most 128 MiB of HBM per device.

v0:
```python
import jax
import jax.numpy as jnp
from jax import lax
from jax.sharding import PartitionSpec as P

EXPERTS = 4
TOP = 2
PATCH_DEV = 128
MOST = 68


def slot_rank(choices):
    total = choices.shape[0]
    hits = (choices[:, :, None] == jnp.arange(EXPERTS, dtype=jnp.int32)[None, None, :]).astype(
        jnp.int32
    )
    blocks = hits.reshape(total // PATCH_DEV, PATCH_DEV * TOP, EXPERTS)
    before = jnp.cumsum(blocks, axis=1) - blocks
    return jnp.sum(before * blocks, axis=2).reshape(total, TOP)


def on_device(
    tokens,
    text_states,
    text_lengths,
    mod_weight,
    router_weight,
    gate_weight,
    up_weight,
    down_weight,
    expert_ids,
    dropped,
):
    img_count, patch_count, width = tokens.shape
    rows = img_count * patch_count
    owners = lax.axis_size("expert")
    split = owners // EXPERTS
    capacity = img_count * MOST
    positions = jnp.arange(text_states.shape[1], dtype=jnp.int32)
    valid = (positions[None, :] < text_lengths[:, None]).astype(jnp.bfloat16)
    pooled = jnp.einsum("it,itc->ic", valid, text_states, preferred_element_type=jnp.float32)
    pooled = (pooled / text_lengths.astype(jnp.float32)[:, None]).astype(jnp.bfloat16)
    partial_value = jnp.dot(pooled, mod_weight, preferred_element_type=jnp.float32)
    summed = lax.psum_scatter(partial_value, "seq", scatter_dimension=0, tiled=True)
    modulation = lax.all_gather(summed, "expert", axis=1, tiled=True)
    scale = modulation[:, :width]
    shift = modulation[:, width:]
    values = tokens.astype(jnp.float32)
    centre = jnp.mean(values, axis=2, keepdims=True)
    spread = jnp.mean((values - centre) ** 2, axis=2, keepdims=True)
    normed = (values - centre) * lax.rsqrt(spread + 1e-06)
    hidden_in = (normed * (1.0 + scale[:, None, :]) + shift[:, None, :]).astype(jnp.bfloat16)
    flat = hidden_in.reshape(rows, width)
    choices = expert_ids.reshape(rows, TOP)
    drop_flat = dropped.reshape(rows, TOP)
    w_gate, w_up, w_down = (
        lax.all_gather(gate_weight, "dp", axis=0, tiled=True),
        lax.all_gather(up_weight, "dp", axis=0, tiled=True),
        lax.all_gather(down_weight, "dp", axis=1, tiled=True),
    )
    expert_now = lax.axis_index("expert") // split
    router_col = lax.dynamic_slice_in_dim(router_weight, expert_now, 1, 1)
    block = (jnp.arange(rows, dtype=jnp.int32) // PATCH_DEV)[:, None]
    slot = block * MOST + slot_rank(choices)
    place = choices * capacity + slot
    row_index = jnp.broadcast_to(jnp.arange(rows, dtype=jnp.int32)[:, None], (rows, TOP))
    source = jnp.where(drop_flat > 0, rows, row_index)
    src_row = (
        jnp.full((EXPERTS * capacity,), rows, jnp.int32)
        .at[place.reshape(-1)]
        .set(source.reshape(-1))
    )
    bins = jnp.take(flat, src_row, axis=0, mode="fill", fill_value=0).reshape(
        EXPERTS, 1, capacity, width
    )
    outgoing = jnp.broadcast_to(bins, (EXPERTS, split, capacity, width)).reshape(
        owners, capacity, width
    )
    binned = lax.all_to_all(outgoing, "expert", split_axis=0, concat_axis=0, tiled=True)
    lined = binned.reshape(-1, width)
    gate_col = jax.nn.sigmoid(jnp.dot(lined, router_col, preferred_element_type=jnp.float32))
    gate = jnp.dot(lined, w_gate, preferred_element_type=jnp.float32)
    upper = jnp.dot(lined, w_up, preferred_element_type=jnp.float32)
    hidden = (jax.nn.silu(gate) * upper).astype(jnp.bfloat16)
    part = jnp.dot(hidden, w_down, preferred_element_type=jnp.float32)
    terms = (part * gate_col).astype(jnp.bfloat16).reshape(binned.shape)
    back = lax.all_to_all(terms, "expert", split_axis=0, concat_axis=0, tiled=True)
    per_expert = back.reshape(EXPERTS, split, capacity, width).astype(jnp.float32).sum(axis=1)
    per_expert = per_expert.reshape(EXPERTS * capacity, width)
    contrib = jnp.take(per_expert, place[:, 0], axis=0) + jnp.take(per_expert, place[:, 1], axis=0)
    result = values + contrib.reshape(img_count, patch_count, width)
    return result.astype(jnp.bfloat16)


def solution(mesh):
    return jax.shard_map(
        on_device,
        mesh=mesh,
        in_specs=(
            P(("dp", "seq"), "expert", None),
            P("dp", None, "seq"),
            P("dp"),
            P("seq", "expert"),
            P(),
            P("dp", "expert"),
            P("dp", "expert"),
            P("expert", "dp"),
            P(("dp", "seq"), "expert", None),
            P(("dp", "seq"), "expert", None),
        ),
        out_specs=P(("dp", "seq"), "expert", None),
        check_vma=False,
    )
```

profile of v0, /device:TPU:6, one launch (start us, length us, event | category | flops | bytes accessed | tf_op | source)
XLA Modules:
  0.0 331.9 jit_solution(1374814211398918187)
XLA Ops:
  6.6 0.7 all-gather.4.cloned.1.call-update
  7.4 0.7 all-gather.6.cloned.1.call-update
  8.1 0.1 copy.23
  8.2 0.1 eq.25
  8.4 1.2 reduce-window.6
  9.8 0.1 copy.25
  9.9 0.1 copy.26
  10.1 0.1 mul.69
  10.3 0.2 add.121
  10.5 0.1 broadcast_in_dim.56
  10.7 0.1 copy.27
  10.8 0.1 gt.12
  11.0 1.4 scatter_custom_fusion
  12.4 0.2 fusion.11
  12.7 0.2 fusion.15
  12.9 32.8 %all-reduce.1 = f32[8,320]{1,0:T(8,128)S(1)} all-reduce(f32[8,320]{1,0:T(8,128)S(1)} %fusion.15), channel_id=2, replica_groups=mesh['dp'=2,'seq'=8,'expert'=16] {'seq'}, use_global_device_ids=true, to_apply=%region_6.7.clone | all-reduce | flops 2560 | bytes 20480
  45.6 0.6 dynamic-slice
  46.9 0.6 dynamic-slice.1
  47.5 0.7 dynamic-slice_reduce_fusion
  48.2 0.3 dynamic-update-slice
  48.4 65.5 %all-reduce = f32[5120]{0:T(1024)S(1)} all-reduce(f32[5120]{0:T(1024)S(1)} %dynamic-update-slice), channel_id=1, replica_groups=mesh['dp'=2,'seq'=8,'expert'=16] {'expert'}, use_global_device_ids=true, to_apply=%add | all-reduce | flops 5120 | bytes 40960
  114.0 0.2 convert_reduce_fusion.1
  114.2 0.3 fusion.4
  114.6 0.5 fusion.9
  115.0 3.1 gather_fusion
  118.1 1.5 gather.10
  119.6 0.1 broadcast_in_dim.57
  119.7 0.2 broadcast_select_fusion
  119.9 3.0 broadcast_in_dim.61
  122.9 24.7 %all-to-all-start = ((bf16[16,68,2560]{2,1,0:T(8,128)(2,1)}), bf16[16,68,2560]{2,1,0:T(8,128)(2,1)}, u32[]{:S(2)}, u32[]{:S(2)}) async-start(bf16[16,68,2560]{2,1,0:T(8,128)(2,1)} %bitcast.37), calls=%async_computation | async-start | bytes 11796480 | tf_op jit(solution)/shard_map/all_to_all | solution.py:79
  147.5 0.2 all-gather.8.cloned.1.call-start
  147.8 0.5 all-gather.8.cloned.1.call-update
  148.3 48.3 %all-to-all-done = bf16[16,68,2560]{2,1,0:T(8,128)(2,1)} async-done(((bf16[16,68,2560]{2,1,0:T(8,128)(2,1)}), bf16[16,68,2560]{2,1,0:T(8,128)(2,1)}, u32[]{:S(2)}, u32[]{:S(2)}) %all-to-all-start) | async-done | bytes 5570592 | tf_op jit(solution)/shard_map/all_to_all | solution.py:79
  196.6 7.9 %reshape.260 = bf16[1088,2560]{1,0:T(8,128)(2,1)} reshape(bf16[16,68,2560]{2,1,0:T(8,128)(2,1)} %all-to-all-done) | data formatting | bytes 11141120 | tf_op jit(solution)/shard_map/reshape | solution.py:80
  204.4 4.1 %convolution_reduce_fusion = f32[1088]{0:T(1024)S(1)} fusion(bf16[1088,2560]{1,0:T(8,128)(2,1)} %reshape.260, bf16[2560,4]{0,1:T(4,128)(2,1)S(1)} %copy-done.4, s32[]{:T(128)S(6)} %select_n.59), kind=kOutput, calls=%fused_computation.21 | convolution fusion | flops 5570560 | bytes 5585156 | tf_op jit(solution)/shard_map/dot_general | solution.py:81
  208.6 10.5 %fusion.26 = f32[1088,864]{1,0:T(8,128)} fusion(bf16[1088,2560]{1,0:T(8,128)(2,1)} %reshape.260, bf16[2560,864]{0,1:T(8,128)(2,1)} %all-gather.4.cloned.1.call-done), kind=kOutput, calls=%fused_computation.70 | convolution fusion | flops 4812963840 | bytes 13754368 | tf_op jit(solution)/shard_map/dot_general | solution.py:82
  219.1 18.5 %fusion = bf16[1088,2560]{1,0:T(8,128)(2,1)} fusion(bf16[864,2560]{1,0:T(8,128)(2,1)} %all-gather.8.cloned.1.call-done, f32[1088]{0:T(1024)S(1)} %add_divide_fusion, bf16[1088,2560]{1,0:T(8,128)(2,1)} %reshape.260, bf16[2560,864]{0,1:T(8,128)(2,1)} %all-gather.6.cloned.1.call-done, f32[1088,864]{1,0:T(8,128)} %fusion.26), kind=kOutput, calls=%fused_computation.6 | convolution fusion | flops 9637138432 | bytes 23752960 | tf_op jit(solution)/shard_map/dot_general | solution.py:85
  237.6 7.9 %reshape.262 = bf16[16,68,2560]{2,1,0:T(8,128)(2,1)} reshape(bf16[1088,2560]{1,0:T(8,128)(2,1)} %fusion) | data formatting | bytes 11141120 | tf_op jit(solution)/shard_map/reshape | solution.py:86
  245.4 7.1 %all-to-all-start.1 = ((bf16[16,68,2560]{2,1,0:T(8,128)(2,1)}), bf16[16,68,2560]{2,1,0:T(8,128)(2,1)}, u32[]{:S(2)}, u32[]{:S(2)}) async-start(bf16[16,68,2560]{2,1,0:T(8,128)(2,1)} %reshape.262), calls=%async_computation.1 | async-start | bytes 11796480 | tf_op jit(solution)/shard_map/all_to_all | solution.py:87
  252.5 0.1 reshape.264
  252.6 0.1 bitcast_add_fusion
  252.7 0.2 slice_reduce_fusion.1
  253.0 53.4 %all-to-all-done.1 = bf16[16,68,2560]{2,1,0:T(8,128)(2,1)} async-done(((bf16[16,68,2560]{2,1,0:T(8,128)(2,1)}), bf16[16,68,2560]{2,1,0:T(8,128)(2,1)}, u32[]{:S(2)}, u32[]{:S(2)}) %all-to-all-start.1) | async-done | bytes 5570592 | tf_op jit(solution)/shard_map/all_to_all | solution.py:87
  306.4 5.5 %convert_reduce_fusion = f32[4,68,2560]{2,1,0:T(8,128)} fusion(bf16[16,68,2560]{2,1,0:T(8,128)(2,1)} %all-to-all-done.1), kind=kLoop, calls=%fused_computation.5 | loop fusion | flops 4874240 | bytes 8355840 | tf_op jit(solution)/shard_map/reduce_sum | solution.py:88
  311.9 3.1 reshape.263
  315.0 3.4 %gather_fusion.1 = f32[128,2560]{1,0:T(8,128)S(1)} fusion(f32[272,2560]{1,0:T(8,128)} %reshape.263, s32[1024]{0:T(1024)S(1)} %pad_clamp_fusion.1), kind=kCustom, calls=%fused_computation.clone | custom fusion | bytes 2621952 | tf_op jit(solution)/shard_map/jit(_take)/gather | solution.py:90
  318.4 4.5 %gather_fusion.2 = f32[128,2560]{1,0:T(8,128)} fusion(f32[272,2560]{1,0:T(8,128)} %reshape.263, s32[1024]{0:T(1024)S(1)} %pad_clamp_fusion), kind=kCustom, calls=%fused_computation.1.clone | custom fusion | bytes 2621952 | tf_op jit(solution)/shard_map/jit(_take)/gather | solution.py:90
  322.9 2.5 fusion.8
  (55 shorter events, 0.7 us)
Async XLA Ops:
  6.5 5.9 %copy-start = (bf16[8,128,512]{2,1,0:T(8,128)(2,1)S(1)}, bf16[8,128,512]{2,1,0:T(8,128)(2,1)}, u32[]{:S(2)}) copy-start(bf16[8,128,512]{2,1,0:T(8,128)(2,1)} %param.13) | copy-start | bytes 3145732
  6.5 1.5 copy-start.5
  6.5 3.2 copy-start.7
  6.5 4.1 %copy-start.6 = (s32[1,128,2]{1,2,0:T(2,128)S(1)}, s32[1,128,2]{1,2,0:T(2,128)}, u32[]{:S(2)}) copy-start(s32[1,128,2]{1,2,0:T(2,128)} %param.21) | copy-start | bytes 3076
  6.5 6.1 %copy-start.3 = (bf16[512,320]{0,1:T(8,128)(2,1)S(1)}, bf16[512,320]{0,1:T(8,128)(2,1)}, u32[]{:S(2)}) copy-start(bf16[512,320]{0,1:T(8,128)(2,1)} %param.15) | copy-start | bytes 983044
  6.5 39.1 %copy-start.9 = (u32[256]{0:T(256)S(1)}, u32[256]{0:T(256)}, u32[]{:S(2)}) copy-start(u32[256]{0:T(256)} %constant.91) | copy-start | bytes 3076
  6.6 40.3 %copy-start.8 = (u32[256]{0:T(256)S(1)}, u32[256]{0:T(256)}, u32[]{:S(2)}) copy-start(u32[256]{0:T(256)} %constant.97) | copy-start | bytes 3076
  6.6 107.4 %copy-start.2 = (bf16[1,128,2560]{2,1,0:T(8,128)(2,1)S(1)}, bf16[1,128,2560]{2,1,0:T(8,128)(2,1)}, u32[]{:S(2)}) copy-start(bf16[1,128,2560]{2,1,0:T(8,128)(2,1)} %param.12) | copy-start | bytes 1966084
  6.6 202.0 %all-gather.4.cloned.1.call-start = ((), (), s32[]{:S(2)}) async-start(), calls=%async_computation.2 | async-start | bytes 6635520 | tf_op jit(solution)/shard_map/all_gather | solution.py:57
  7.3 211.8 %all-gather.6.cloned.1.call-start = ((), (), s32[]{:S(2)}) async-start(), calls=%async_computation.3 | async-start | bytes 6635520 | tf_op jit(solution)/shard_map/all_gather | solution.py:58
  122.9 73.7 %all-to-all-start = ((bf16[16,68,2560]{2,1,0:T(8,128)(2,1)}), bf16[16,68,2560]{2,1,0:T(8,128)(2,1)}, u32[]{:S(2)}, u32[]{:S(2)}) async-start(bf16[16,68,2560]{2,1,0:T(8,128)(2,1)} %bitcast.37), calls=%async_computation | async-start | bytes 11796480 | tf_op jit(solution)/shard_map/all_to_all | solution.py:79
  147.5 71.6 %all-gather.8.cloned.1.call-start = ((), (), s32[]{:S(2)}) async-start(), calls=%async_computation.4 | async-start | bytes 6635520 | tf_op jit(solution)/shard_map/all_gather | solution.py:59
  148.3 56.1 %copy-start.4 = (bf16[2560,4]{0,1:T(4,128)(2,1)S(1)}, bf16[2560,4]{0,1:T(4,128)(2,1)}, u32[]{:S(2)}) copy-start(bf16[2560,4]{0,1:T(4,128)(2,1)} %param.16) | copy-start | bytes 61444
  245.4 60.9 %all-to-all-start.1 = ((bf16[16,68,2560]{2,1,0:T(8,128)(2,1)}), bf16[16,68,2560]{2,1,0:T(8,128)(2,1)}, u32[]{:S(2)}, u32[]{:S(2)}) async-start(bf16[16,68,2560]{2,1,0:T(8,128)(2,1)} %reshape.262), calls=%async_computation.1 | async-start | bytes 11796480 | tf_op jit(solution)/shard_map/all_to_all | solution.py:87
  318.4 7.0 %copy-start.1 = (bf16[8,128,512]{2,1,0:T(8,128)(2,1)S(1)}, bf16[8,128,512]{2,1,0:T(8,128)(2,1)}, u32[]{:S(2)}) copy-start(bf16[8,128,512]{2,1,0:T(8,128)(2,1)} %param.13) | copy-start | bytes 3145732
Sparse Core Ops, SparseCore 0:
  9.2 22.2 all-gather.3
  33.3 20.6 all-gather.5
  150.2 17.2 all-gather.7
where the time goes:
time: 333 us; the launch traced here: 332 us
  waiting for transfers between devices  104 us (31%)
  blocking collectives  98.3 us (30%)
  local copies, waits for them, and re-layouts  39.7 us (12%)
  matrix products  33.5 us (10%)
  starting transfers between devices  32 us (10%)
  between operations  14.1 us (4%)
  other arithmetic  10.7 us (3%)
    unnamed x2, blocking collectives  98.3 us
    all_to_all x1, waiting for transfers between devices, on_device(): lax.all_to_all(terms, 'expert', split_axis=0, concat_axis=0, tiled=True)  53.4 us
    all_to_all x1, waiting for transfers between devices, on_device(): lax.all_to_all(outgoing, 'expert', split_axis=0, concat_axis=0, tiled=True)  48.3 us
    all_to_all x1, starting transfers between devices, on_device(): lax.all_to_all(outgoing, 'expert', split_axis=0, concat_axis=0, tiled=True)  24.7 us
    dot_general x1, matrix products, on_device(): part = jnp.dot(hidden, w_down, preferred_element_type=jnp.float32)  18.5 us
    dot_general x1, matrix products, on_device(): gate = jnp.dot(lined, w_gate, preferred_element_type=jnp.float32)  10.5 us
    reshape x1, local copies, waits for them, and re-layouts, on_device(): terms = (part * gate_col).astype(jnp.bfloat16).reshape(binned.shape)  7.86 us
    reshape x1, local copies, waits for them, and re-layouts, on_device(): lined = binned.reshape(-1, width)  7.85 us
  transfers between devices with their start and end apart: 5, of which 2 were waited for; matrix products, arithmetic and copies ran while one was open for 12% of the time, Pallas kernels for 0%

commit v1 on v0

v1 whole, which is shorter than its diff:
```python
import functools

import jax
import jax.numpy as jnp
from jax import lax
from jax.experimental import pallas as pl
from jax.experimental.pallas import tpu as pltpu
from jax.sharding import PartitionSpec as P

SIDE = 4
SLOTS = 72
CHUNKS = ((0,), (1, -1, 2))
OFFSETS = (0, 1, -1, 2)
VMEM_LIMIT = 56 * 1024 * 1024


def along_x(step):
    return [
        (y * SIDE + x, y * SIDE + (x + step) % SIDE) for y in range(SIDE) for x in range(SIDE)
    ]


def along_y(step):
    return [
        (y * SIDE + x, ((y + step) % SIDE) * SIDE + x) for y in range(SIDE) for x in range(SIDE)
    ]


def shift(value, perm):
    return lax.ppermute(value, "expert", perm)


def bin_kernel(y_ref, ids_ref, tokens_ref, normed_ref, *bin_refs):
    rows, width = tokens_ref.shape
    for start in range(0, rows, 16):
        block = tokens_ref[start : start + 16, :].astype(jnp.float32)
        centre = jnp.sum(block, axis=1, keepdims=True) * (1.0 / width)
        block = block - centre
        spread = jnp.sum(block * block, axis=1, keepdims=True) * (1.0 / width)
        normed_ref[start : start + 16, :] = (block * lax.rsqrt(spread + 1e-06)).astype(
            jnp.bfloat16
        )
    before = (
        lax.broadcasted_iota(jnp.int32, (rows, rows), 0)
        < lax.broadcasted_iota(jnp.int32, (rows, rows), 1)
    ).astype(jnp.bfloat16)
    slot = lax.broadcasted_iota(jnp.int32, (SLOTS, rows), 0)
    normed = normed_ref[...]
    for offset, bin_ref in zip(OFFSETS, bin_refs):
        expert = lax.rem(y_ref[0] + offset + SIDE, SIDE)
        named = jnp.max((ids_ref[...] == expert).astype(jnp.float32), axis=0, keepdims=True)
        rank = jnp.dot(
            jnp.broadcast_to(named, (16, rows)).astype(jnp.bfloat16),
            before,
            preferred_element_type=jnp.float32,
        )[0:1, :].astype(jnp.int32)
        pick = jnp.where((slot == rank) & (named > 0.0), 1.0, 0.0).astype(jnp.bfloat16)
        bin_ref[...] = jnp.dot(pick, normed, preferred_element_type=jnp.float32).astype(
            jnp.bfloat16
        )


def make_bins(y_index, ids_rows, tokens):
    rows, width = tokens.shape
    vmem = pl.BlockSpec(memory_space=pltpu.VMEM)
    return pl.pallas_call(
        bin_kernel,
        out_shape=[jax.ShapeDtypeStruct((rows, width), jnp.bfloat16)]
        + [jax.ShapeDtypeStruct((SLOTS, width), jnp.bfloat16)] * len(OFFSETS),
        in_specs=[pl.BlockSpec(memory_space=pltpu.SMEM), vmem, vmem],
        out_specs=[vmem] * (1 + len(OFFSETS)),
        compiler_params=pltpu.CompilerParams(vmem_limit_bytes=VMEM_LIMIT),
        cost_estimate=pl.CostEstimate(
            flops=2 * 4 * SLOTS * rows * width, bytes_accessed=8 * rows * width, transcendentals=0
        ),
        name="normalise_and_bin",
    )(y_index, ids_rows, tokens)


def expert_kernel(
    dp_ref,
    mod_ref,
    own_ref,
    left_ref,
    right_ref,
    far_a_ref,
    far_b_ref,
    gate_own,
    gate_far,
    up_own,
    up_far,
    down_own,
    down_far,
    out_own,
    out_left,
    out_right,
    out_far_a,
    out_far_b,
    w_gate,
    w_up,
    w_down,
    acc_gate,
    acc_up,
    sems,
):
    width = own_ref.shape[2]
    half = width // 2
    tile = half // 2
    first = pl.program_id(0) == 0
    dp = dp_ref[0]

    def pieces():
        for part in range(4):
            bank, start = part // 2, (part % 2) * tile
            yield bank, gate_own, gate_far, w_gate, 0, pl.ds(start, tile), part
            yield bank, up_own, up_far, w_up, 0, pl.ds(start, tile), part
        for part in range(4):
            bank, start = part // 2, (part % 2) * tile
            yield bank, down_own, down_far, w_down, 1, pl.ds(start, tile), part

    def copies(source):
        for number, (bank, own, far, scratch, axis, span, part) in enumerate(pieces()):
            ref = (own if source == "own" else far) if source != "bank" else own
            index = (span, slice(None)) if axis == 0 else (slice(None), span)
            yield (
                number,
                bank,
                pltpu.make_async_copy(
                    ref.at[index], scratch.at[(bank,) + index], sems.at[number]
                ),
            )

    @pl.when(first)
    def _():
        for (number, bank, mine), (_, _, other) in zip(copies("own"), copies("far")):
            is_mine = dp == bank

            @pl.when(is_mine)
            def _(mine=mine):
                mine.start()

            @pl.when(jnp.logical_not(is_mine))
            def _(other=other):
                other.start()

    waits = [copy for _, _, copy in copies("own")]

    for part in range(4):

        @pl.when(first)
        def _(part=part):
            waits[2 * part].wait()
            waits[2 * part + 1].wait()

        bank, start = part // 2, (part % 2) * tile
        span = slice(part * tile, (part + 1) * tile)
        far_ref = far_a_ref if bank == 0 else far_b_ref
        values = jnp.concatenate(
            [
                own_ref[0, :, span].astype(jnp.float32),
                left_ref[0, :, span].astype(jnp.float32),
                right_ref[0, :, span].astype(jnp.float32),
                far_ref[0, :, start : start + tile].astype(jnp.float32),
            ],
            axis=0,
        )
        hidden_in = (values * (1.0 + mod_ref[0:1, span]) + mod_ref[1:2, span]).astype(jnp.bfloat16)
        gate = jnp.dot(
            hidden_in, w_gate[bank, start : start + tile, :], preferred_element_type=jnp.float32
        )
        upper = jnp.dot(
            hidden_in, w_up[bank, start : start + tile, :], preferred_element_type=jnp.float32
        )
        if part == 0:
            acc_gate[...] = gate
            acc_up[...] = upper
        else:
            acc_gate[...] += gate
            acc_up[...] += upper
    hidden = (jax.nn.silu(acc_gate[...]) * acc_up[...]).astype(jnp.bfloat16)
    for part in range(4):

        @pl.when(first)
        def _(part=part):
            waits[8 + part].wait()

        bank, start = part // 2, (part % 2) * tile
        span = slice(part * tile, (part + 1) * tile)
        out = jnp.dot(
            hidden, w_down[bank, :, start : start + tile], preferred_element_type=jnp.float32
        )
        out_own[0, :, span] = out[0:SLOTS].astype(jnp.bfloat16)
        out_left[0, :, span] = out[SLOTS : 2 * SLOTS].astype(jnp.bfloat16)
        out_right[0, :, span] = out[2 * SLOTS : 3 * SLOTS].astype(jnp.bfloat16)
        out_far = out_far_a if bank == 0 else out_far_b
        out_far[0, :, start : start + tile] = out[3 * SLOTS : 4 * SLOTS].astype(jnp.bfloat16)


def run_expert(dp_index, modulation, own, left, right, far_a, far_b, weights):
    count, slots, width = own.shape
    half = width // 2
    units = weights[0].shape[1]
    any_space = pl.BlockSpec(memory_space=pl.ANY)
    whole = pl.BlockSpec((1, slots, width), lambda i: (i, 0, 0))
    split = pl.BlockSpec((1, slots, half), lambda i: (i, 0, 0))
    wide = jax.ShapeDtypeStruct((count, slots, width), jnp.bfloat16)
    narrow = jax.ShapeDtypeStruct((count, slots, half), jnp.bfloat16)
    rows = SIDE * slots
    return pl.pallas_call(
        expert_kernel,
        grid=(count,),
        out_shape=[wide, wide, wide, narrow, narrow],
        in_specs=[
            pl.BlockSpec(memory_space=pltpu.SMEM),
            pl.BlockSpec((2, width), lambda i: (0, 0)),
            whole,
            whole,
            whole,
            split,
            split,
        ]
        + [any_space] * 6,
        out_specs=[whole, whole, whole, split, split],
        scratch_shapes=[
            pltpu.VMEM((2, half, units), jnp.bfloat16),
            pltpu.VMEM((2, half, units), jnp.bfloat16),
            pltpu.VMEM((2, units, half), jnp.bfloat16),
            pltpu.VMEM((rows, units), jnp.float32),
            pltpu.VMEM((rows, units), jnp.float32),
            pltpu.SemaphoreType.DMA((12,)),
        ],
        compiler_params=pltpu.CompilerParams(vmem_limit_bytes=VMEM_LIMIT),
        cost_estimate=pl.CostEstimate(
            flops=count * rows * width * units * 6,
            bytes_accessed=width * units * 6 + count * rows * width * 4,
            transcendentals=count * rows * units,
        ),
        name="expert_units",
    )(dp_index, modulation, own, left, right, far_a, far_b, *weights)


def combine_kernel(
    y_ref, ids_ref, dropped_ref, tokens_ref, normed_ref, mod_ref, router_ref, *refs
):
    back_refs, out_ref = refs[:-1], refs[-1]
    rows, width = tokens_ref.shape
    hidden_in = (
        normed_ref[...].astype(jnp.float32) * (1.0 + mod_ref[0:1, :]) + mod_ref[1:2, :]
    ).astype(jnp.bfloat16)
    gates = jax.nn.sigmoid(
        jnp.dot(hidden_in, router_ref[...], preferred_element_type=jnp.float32)
    )
    row = lax.broadcasted_iota(jnp.int32, (rows, rows), 0)
    column = lax.broadcasted_iota(jnp.int32, (rows, rows), 1)
    before = (column < row).astype(jnp.bfloat16)
    lane = lax.broadcasted_iota(jnp.int32, (rows, SLOTS), 1)
    experts = lax.broadcasted_iota(jnp.int32, gates.shape, 1)
    kept = 1.0 - dropped_ref[...].astype(jnp.float32)
    picks, scales = [], []
    for offset in OFFSETS:
        expert = lax.rem(y_ref[0] + offset + SIDE, SIDE)
        match = (ids_ref[...] == expert).astype(jnp.float32)
        named = jnp.max(match, axis=1, keepdims=True)
        weight = jnp.sum(match * kept, axis=1, keepdims=True) * jnp.sum(
            jnp.where(experts == expert, gates, 0.0), axis=1, keepdims=True
        )
        rank = jnp.dot(
            before,
            jnp.broadcast_to(named, (rows, 128)).astype(jnp.bfloat16),
            preferred_element_type=jnp.float32,
        )[:, 0:1].astype(jnp.int32)
        picks.append(jnp.where((lane == rank) & (named > 0.0), 1.0, 0.0).astype(jnp.bfloat16))
        scales.append(weight)
    tile = width // 4
    for start in range(0, width, tile):
        total = tokens_ref[:, start : start + tile].astype(jnp.float32)
        for pick, weight, back_ref in zip(picks, scales, back_refs):
            total = total + weight * jnp.dot(
                pick, back_ref[:, start : start + tile], preferred_element_type=jnp.float32
            )
        out_ref[:, start : start + tile] = total.astype(jnp.bfloat16)


def combine(y_index, ids, dropped, tokens, normed, modulation, router, backs):
    rows, width = tokens.shape
    vmem = pl.BlockSpec(memory_space=pltpu.VMEM)
    return pl.pallas_call(
        combine_kernel,
        out_shape=jax.ShapeDtypeStruct((rows, width), jnp.bfloat16),
        in_specs=[pl.BlockSpec(memory_space=pltpu.SMEM)] + [vmem] * (6 + len(backs)),
        out_specs=vmem,
        compiler_params=pltpu.CompilerParams(vmem_limit_bytes=VMEM_LIMIT),
        cost_estimate=pl.CostEstimate(
            flops=2 * 4 * SLOTS * rows * width, bytes_accessed=10 * rows * width, transcendentals=0
        ),
        name="weigh_and_add",
    )(y_index, ids, dropped, tokens, normed, modulation, router, *backs)


def on_device(
    tokens,
    text_states,
    text_lengths,
    mod_weight,
    router_weight,
    gate_weight,
    up_weight,
    down_weight,
    expert_ids,
    dropped,
):
    _, rows, width = tokens.shape
    half = width // 2
    tokens = tokens[0]
    ids = expert_ids[0]
    y_index = (lax.axis_index("expert") // SIDE).astype(jnp.int32).reshape(1)
    dp_index = lax.axis_index("dp").astype(jnp.int32).reshape(1)

    normed, *bins = make_bins(y_index, ids.T, tokens)
    bins = dict(zip(OFFSETS, bins))

    swap = [(0, 1), (1, 0)]
    weights = []
    for own in (gate_weight, up_weight, down_weight):
        weights += [own, lax.ppermute(own, "dp", swap)]

    positions = jnp.arange(text_states.shape[1], dtype=jnp.int32)
    valid = (positions[None, :] < text_lengths[:, None]).astype(jnp.bfloat16)
    pooled = jnp.einsum("it,itc->ic", valid, text_states, preferred_element_type=jnp.float32)
    pooled = (pooled / text_lengths.astype(jnp.float32)[:, None]).astype(jnp.bfloat16)
    partial_value = jnp.dot(pooled, mod_weight, preferred_element_type=jnp.float32)
    spread = lax.all_to_all(partial_value, "seq", split_axis=0, concat_axis=0, tiled=True)
    columns = jnp.sum(spread, axis=0, keepdims=True)
    owners = lax.axis_size("expert")
    modulation = lax.all_to_all(
        jnp.broadcast_to(columns, (owners, columns.shape[1])),
        "expert",
        split_axis=0,
        concat_axis=0,
        tiled=True,
    ).reshape(2, width)

    arrived = {
        offset: bins[offset] if offset == 0 else shift(bins[offset], along_y(offset))
        for offset in OFFSETS
    }
    backs = {}
    for chunk in CHUNKS:
        own = jnp.stack([arrived[offset] for offset in chunk])
        left = shift(own, along_x(1))
        right = shift(own, along_x(-1))
        far_a = shift(left[:, :, :half], along_x(1))
        far_b = shift(right[:, :, half:], along_x(-1))
        out_own, out_left, out_right, out_far_a, out_far_b = run_expert(
            dp_index, modulation, own, left, right, far_a, far_b, weights
        )
        got_a = shift(out_far_a, along_x(-1))
        got_b = shift(out_far_b, along_x(1))
        out_left = jnp.concatenate([out_left[:, :, :half] + got_a, out_left[:, :, half:]], axis=2)
        out_right = jnp.concatenate(
            [out_right[:, :, :half], out_right[:, :, half:] + got_b], axis=2
        )
        from_right = shift(out_left, along_x(-1))
        from_left = shift(out_right, along_x(1))
        summed = (
            out_own.astype(jnp.float32)
            + from_right.astype(jnp.float32)
            + from_left.astype(jnp.float32)
        ).astype(jnp.bfloat16)
        for place, offset in enumerate(chunk):
            piece = summed[place]
            backs[offset] = piece if offset == 0 else shift(piece, along_y(-offset))
    result = combine(
        y_index,
        ids,
        dropped[0],
        tokens,
        normed,
        modulation,
        router_weight,
        [backs[offset] for offset in OFFSETS],
    )
    return result[None]


def solution(mesh):
    return jax.shard_map(
        on_device,
        mesh=mesh,
        in_specs=(
            P(("dp", "seq"), "expert", None),
            P("dp", None, "seq"),
            P("dp"),
            P("seq", "expert"),
            P(),
            P("dp", "expert"),
            P("dp", "expert"),
            P("expert", "dp"),
            P(("dp", "seq"), "expert", None),
            P(("dp", "seq"), "expert", None),
        ),
        out_specs=P(("dp", "seq"), "expert", None),
        check_vma=False,
    )
```

time: 333 us -> 217 us (0.65)
  blocking collectives: 98.3 us -> 11.6 us
  Pallas kernels: 0 us -> 44 us
  matrix products: 33.5 us -> 0.43 us
  waiting for transfers between devices: 104 us -> 77.9 us
  starting transfers between devices: 32 us -> 52.7 us
  local copies, waits for them, and re-layouts: 39.7 us -> 25.8 us
  between operations: 14.1 us -> 0.3 us
  other arithmetic: 10.7 us -> 2.2 us
    all_to_all x2 -> x1, waiting for transfers between devices: 102 us -> 0.01 us  [on_device(): lax.all_to_all(jnp.broadcast_to(columns, (owners, columns.shape[1])), 'ex...]
    unnamed x2 -> x0, blocking collectives: 98.3 us -> none
    ppermute x0 -> x25, waiting for transfers between devices: none -> 77.9 us  [the longest x22 77.9 us: shift(): return lax.ppermute(value, 'expert', perm)]
    pallas_call x0 -> x4, Pallas kernels: none -> 44 us  [the longest x2 36.7 us: run_expert(): pl.pallas_call(expert_kernel, grid=(count,), out_shape=[wide, wide, wide,...]
    ppermute x0 -> x25, starting transfers between devices: none -> 43.5 us  [the longest x22 43 us: shift(): return lax.ppermute(value, 'expert', perm)]
    dot_general x3 -> x0, matrix products: 33.1 us -> none  [the longest x1 18.5 us: on_device(): part = jnp.dot(hidden, w_down, preferred_element_type=jnp.float32)]
    all_to_all x2 -> x1, starting transfers between devices: 31.7 us -> 9.23 us  [on_device(): lax.all_to_all(jnp.broadcast_to(columns, (owners, columns.shape[1])), 'ex...]
    reshape x5 -> x1, local copies, waits for them, and re-layouts: 18.9 us -> 0.68 us  [on_device(): modulation = lax.all_to_all(jnp.broadcast_to(columns, (owners, columns.sh...]
  transfers between devices with their start and end apart: 5 -> 26, of which waited for: 2 -> 10; matrix products, arithmetic and copies ran while one was open for 12% -> 12% of each run, Pallas kernels for 0% -> 19%
where the time goes in v1:
time: 217 us; the launch traced here: 215 us
  waiting for transfers between devices  77.9 us (36%)
  starting transfers between devices  52.7 us (24%)
  Pallas kernels  44 us (20%)
  local copies, waits for them, and re-layouts  25.8 us (12%)
  blocking collectives  11.6 us (5%)
  other arithmetic  2.2 us (1%)
    ppermute x22, waiting for transfers between devices, shift(): return lax.ppermute(value, 'expert', perm)  77.9 us
    ppermute x22, starting transfers between devices, shift(): return lax.ppermute(value, 'expert', perm)  43 us
    pallas_call x2, Pallas kernels, run_expert(): pl.pallas_call(expert_kernel, grid=(count,), out_shape=[wide, wide, wide,...  36.7 us
    unnamed x51, local copies, waits for them, and re-layouts  12 us
    all_to_all x1, blocking collectives, on_device(): lax.all_to_all(partial_value, 'seq', split_axis=0, concat_axis=0, tiled=T...  11.6 us
    all_to_all x1, starting transfers between devices, on_device(): lax.all_to_all(jnp.broadcast_to(columns, (owners, columns.shape[1])), 'ex...  9.23 us
    ppermute x2, local copies, waits for them, and re-layouts, on_device(): weights += [own, lax.ppermute(own, 'dp', swap)]  8.72 us
  transfers between devices with their start and end apart: 26, of which 10 were waited for; matrix products, arithmetic and copies ran while one was open for 12% of the time, Pallas kernels for 19%

profile of v1, /device:TPU:6, one launch (start us, length us, event | category | flops | bytes accessed | tf_op | source)
XLA Modules:
  0.0 215.0 jit_solution(10345920120591587622)
XLA Ops:
  0.5 0.8 copy.21
  1.3 0.6 copy.23.ids_ref
  1.9 3.2 %normalise_and_bin.1 = (bf16[128,2560]{1,0:T(8,128)(2,1)}, bf16[72,2560]{1,0:T(8,128)(2,1)}, bf16[72,2560]{1,0:T(8,128)(2,1)}, bf16[72,2560]{1,0:T(8,128)(2,1)}, bf16[72,2560]{1,0:T(8,128)(2,1)}) custom-call(s32[1]{0:T(128)} %bitcast.y_ref, s32[2,128]{1,0:T(2,128)} %copy.23.ids_ref, bf16[128,2560]{1,0:T(8,128)(2,1)} %bitcast.31), custom_call_target="tpu_custom_call" | custom-call | flops 188743680 | bytes 2621440 | tf_op jit(solution)/shard_map/normalise_and_bin/pallas_call | solution.py:66
  5.2 1.6 collective-permute-start.11
  6.7 1.7 collective-permute-start.12
  8.4 2.0 collective-permute-start.13
  10.4 6.8 %collective-permute-done.11 = bf16[72,2560]{1,0:T(8,128)(2,1)S(1)} collective-permute-done((bf16[72,2560]{1,0:T(8,128)(2,1)}, bf16[72,2560]{1,0:T(8,128)(2,1)S(1)}, u32[]{:S(2)}, u32[]{:S(2)}) %collective-permute-start.11) | collective-permute-done | bytes 368672 | tf_op jit(solution)/shard_map/ppermute | solution.py:30
  17.2 1.2 collective-permute-done.12
  18.4 8.8 %collective-permute-start = (bf16[1,72,2560]{2,1,0:T(8,128)(2,1)}, bf16[1,72,2560]{2,1,0:T(8,128)(2,1)S(1)}, u32[]{:S(2)}, u32[]{:S(2)}) collective-permute-start(bf16[1,72,2560]{2,1,0:T(8,128)(2,1)} %bitcast.38), channel_id=1, source_target_pairs={{0,1},{1,2},{2,3},{3,0},{4,5},{5,6},{6,7},{7,4},{8,9},{9,10},{10,1... | collective-permute-start | bytes 1105928 | tf_op jit(solution)/shard_map/ppermute | solution.py:30
  27.4 8.7 %collective-permute-done.left_ref = bf16[1,72,2560]{2,1,0:T(8,128)(2,1)S(1)} collective-permute-done((bf16[1,72,2560]{2,1,0:T(8,128)(2,1)}, bf16[1,72,2560]{2,1,0:T(8,128)(2,1)S(1)}, u32[]{:S(2)}, u32[]{:S(2)}) %collective-permute-start) | collective-permute-done | bytes 368672 | tf_op jit(solution)/shard_map/ppermute | solution.py:30
  36.0 3.6 %collective-permute-start.14 = (bf16[3,72,2560]{2,1,0:T(8,128)(2,1)S(1)}, bf16[3,72,2560]{2,1,0:T(8,128)(2,1)S(1)}, u32[]{:S(2)}, u32[]{:S(2)}) collective-permute-start(bf16[3,72,2560]{2,1,0:T(8,128)(2,1)S(1)} %pad_maximum_fusion.own_ref), channel_id=1, source_target_pairs={{0,1},{1,2},{2,3},{3,0},{4,5},{5,6},{6,7},{7,4},{8,9},{9,10},{10,1... | collective-permute-start | bytes 3317768 | tf_op jit(solution)/shard_map/ppermute | solution.py:30
  39.7 0.7 slice.60
  40.4 0.7 slice.61
  41.1 22.0 %collective-permute-done.14.left_ref = bf16[3,72,2560]{2,1,0:T(8,128)(2,1)S(1)} collective-permute-done((bf16[3,72,2560]{2,1,0:T(8,128)(2,1)S(1)}, bf16[3,72,2560]{2,1,0:T(8,128)(2,1)S(1)}, u32[]{:S(2)}, u32[]{:S(2)}) %collective-permute-start.14) | collective-permute-done | bytes 1105952 | tf_op jit(solution)/shard_map/ppermute | solution.py:30
  63.2 3.7 %collective-permute-start.2 = (bf16[1,72,1280]{2,1,0:T(8,128)(2,1)}, bf16[1,72,1280]{2,1,0:T(8,128)(2,1)S(1)}, u32[]{:S(2)}, u32[]{:S(2)}) collective-permute-start(bf16[1,72,1280]{2,1,0:T(8,128)(2,1)} %slice.60), channel_id=1, source_target_pairs={{0,1},{1,2},{2,3},{3,0},{4,5},{5,6},{6,7},{7,4},{8,9},{9,10},{10,1... | collective-permute-start | bytes 552968 | tf_op jit(solution)/shard_map/ppermute | solution.py:30
  66.8 0.8 slice.62
  67.7 0.8 slice.63
  68.5 3.3 %collective-permute-start.16 = (bf16[3,72,1280]{2,1,0:T(8,128)(2,1)}, bf16[3,72,1280]{2,1,0:T(8,128)(2,1)}, u32[]{:S(2)}, u32[]{:S(2)}) collective-permute-start(bf16[3,72,1280]{2,1,0:T(8,128)(2,1)} %slice.62), channel_id=1, source_target_pairs={{0,1},{1,2},{2,3},{3,0},{4,5},{5,6},{6,7},{7,4},{8,9},{9,10},{10,1... | collective-permute-start | bytes 1658888 | tf_op jit(solution)/shard_map/ppermute | solution.py:30
  72.4 11.6 %all_to_all.15 = f32[8,1,320]{2,1,0:T(1,128)S(1)} all-to-all(f32[8,1,320]{2,1,0:T(1,128)S(1)} %copy.24), channel_id=1, replica_groups=mesh['dp'=2,'seq'=8,'expert'=16] {'seq'}, dimensions={0} | all-to-all | bytes 20480 | tf_op jit(solution)/shard_map/all_to_all | solution.py:332
  84.0 0.6 broadcast_in_dim.4
  84.6 9.2 %all-to-all-start.1 = ((f32[16,1,320]{2,1,0:T(1,128)}), f32[16,1,320]{2,1,0:T(1,128)S(1)}, u32[]{:S(2)}, u32[]{:S(2)}) async-start(f32[16,1,320]{2,1,0:T(1,128)} %broadcast_in_dim.4), calls=%async_computation.1 | async-start | bytes 49152 | tf_op jit(solution)/shard_map/all_to_all | solution.py:335
  93.9 3.3 %copy.25.gate_own = bf16[1280,864]{1,0:T(8,128)(2,1)} copy(bf16[1280,864]{0,1:T(8,128)(2,1)S(1)} %copy-done.1) | data formatting | bytes 4423680 | tf_op args[5]
  97.2 4.3 %copy.27.up_own = bf16[1280,864]{1,0:T(8,128)(2,1)} copy(bf16[1280,864]{0,1:T(8,128)(2,1)} %param.16) | data formatting | bytes 4423680 | tf_op args[6]
  101.6 0.7 reshape.21.mod_ref
  102.3 4.3 %copy.26.gate_far = bf16[1280,864]{1,0:T(8,128)(2,1)} copy(bf16[1280,864]{0,1:T(8,128)(2,1)} %collective-permute-done.4) | data formatting | bytes 4423680 | tf_op jit(solution)/shard_map/ppermute | solution.py:325
  106.6 4.4 %copy.28.up_far = bf16[1280,864]{1,0:T(8,128)(2,1)} copy(bf16[1280,864]{0,1:T(8,128)(2,1)} %collective-permute-done.5) | data formatting | bytes 4423680 | tf_op jit(solution)/shard_map/ppermute | solution.py:325
  111.0 0.7 copy-done.18
  111.7 11.1 %expert_units.2 = (bf16[1,72,2560]{2,1,0:T(8,128)(2,1)}, bf16[1,72,2560]{2,1,0:T(8,128)(2,1)}, bf16[1,72,2560]{2,1,0:T(8,128)(2,1)}, bf16[1,72,1280]{2,1,0:T(8,128)(2,1)}, bf16[1,72,1280]{2,1,0:T(8,128)(2,1)}) custom-call(s32[1]{0:T(128)} %bitcast.8.dp_ref, f32[2,2560]{1,0:T(2,128)} %reshape.21.mod_ref, bf16[1,72,2560]{2,1,0:T(8,128)(2,1)} %bitcast.40, ...), custom_call_target="tpu_custom_call" | custom-call | flops 3822059520 | bytes 16220160 | tf_op jit(solution)/shard_map/expert_units/pallas_call | solution.py:209
  122.8 1.2 collective-permute-start.7
  124.0 25.6 %expert_units.3 = (bf16[3,72,2560]{2,1,0:T(8,128)(2,1)}, bf16[3,72,2560]{2,1,0:T(8,128)(2,1)}, bf16[3,72,2560]{2,1,0:T(8,128)(2,1)}, bf16[3,72,1280]{2,1,0:T(8,128)(2,1)}, bf16[3,72,1280]{2,1,0:T(8,128)(2,1)}) custom-call(s32[1]{0:T(128)} %bitcast.8.dp_ref, f32[2,2560]{1,0:T(2,128)} %reshape.21.mod_ref, bf16[3,72,2560]{2,1,0:T(8,128)(2,1)} %copy-done.2, ...), custom_call_target="tpu_custom_call" | custom-call | flops 11466178560 | bytes 22118400 | tf_op jit(solution)/shard_map/expert_units/pallas_call | solution.py:209
  149.6 0.6 collective-permute-start.18
  150.2 1.2 copy.33.router_ref
  151.4 0.7 copy.22
  152.1 2.7 %collective-permute-start.20 = (bf16[3,72,1280]{2,1,0:T(8,128)(2,1)}, bf16[3,72,1280]{2,1,0:T(8,128)(2,1)S(1)}, u32[]{:S(2)}, u32[]{:S(2)}) collective-permute-start(bf16[3,72,1280]{2,1,0:T(8,128)(2,1)} %get-tuple-element.34), channel_id=1, source_target_pairs={{0,1},{1,2},{2,3},{3,0},{4,5},{5,6},{6,7},{7,4},{8,9},{9,10},{10,1... | collective-permute-start | bytes 1658888 | tf_op jit(solution)/shard_map/ppermute | solution.py:30
  154.8 1.2 collective-permute-start.9
  156.0 6.2 %collective-permute-done.18 = bf16[3,72,1280]{2,1,0:T(8,128)(2,1)S(1)} collective-permute-done((bf16[3,72,1280]{2,1,0:T(8,128)(2,1)}, bf16[3,72,1280]{2,1,0:T(8,128)(2,1)S(1)}, u32[]{:S(2)}, u32[]{:S(2)}) %collective-permute-start.18) | collective-permute-done | bytes 552992 | tf_op jit(solution)/shard_map/ppermute | solution.py:30
  162.6 5.2 %collective-permute-done.20 = bf16[3,72,1280]{2,1,0:T(8,128)(2,1)S(1)} collective-permute-done((bf16[3,72,1280]{2,1,0:T(8,128)(2,1)}, bf16[3,72,1280]{2,1,0:T(8,128)(2,1)S(1)}, u32[]{:S(2)}, u32[]{:S(2)}) %collective-permute-start.20) | collective-permute-done | bytes 552992 | tf_op jit(solution)/shard_map/ppermute | solution.py:30
  168.0 3.6 %collective-permute-start.21 = (bf16[3,72,2560]{2,1,0:T(8,128)(2,1)S(1)}, bf16[3,72,2560]{2,1,0:T(8,128)(2,1)S(1)}, u32[]{:S(2)}, u32[]{:S(2)}) collective-permute-start(bf16[3,72,2560]{2,1,0:T(8,128)(2,1)S(1)} %pad_maximum_fusion.2), channel_id=1, source_target_pairs={{0,1},{1,2},{2,3},{3,0},{4,5},{5,6},{6,7},{7,4},{8,9},{9,10},{10,1... | collective-permute-start | bytes 3317768 | tf_op jit(solution)/shard_map/ppermute | solution.py:30
  171.9 3.6 %collective-permute-start.10 = (bf16[1,72,2560]{2,1,0:T(8,128)(2,1)S(1)}, bf16[1,72,2560]{2,1,0:T(8,128)(2,1)S(1)}, u32[]{:S(2)}, u32[]{:S(2)}) collective-permute-start(bf16[1,72,2560]{2,1,0:T(8,128)(2,1)S(1)} %pad_maximum_fusion.4), channel_id=1, source_target_pairs={{0,1},{1,2},{2,3},{3,0},{4,5},{5,6},{6,7},{7,4},{8,9},{9,10},{10,1... | collective-permute-start | bytes 1105928 | tf_op jit(solution)/shard_map/ppermute | solution.py:30
  175.5 13.1 %collective-permute-done.19 = bf16[3,72,2560]{2,1,0:T(8,128)(2,1)S(1)} collective-permute-done((bf16[3,72,2560]{2,1,0:T(8,128)(2,1)S(1)}, bf16[3,72,2560]{2,1,0:T(8,128)(2,1)S(1)}, u32[]{:S(2)}, u32[]{:S(2)}) %collective-permute-start.19) | collective-permute-done | bytes 1105952 | tf_op jit(solution)/shard_map/ppermute | solution.py:30
  188.6 5.1 %collective-permute-done.21 = bf16[3,72,2560]{2,1,0:T(8,128)(2,1)S(1)} collective-permute-done((bf16[3,72,2560]{2,1,0:T(8,128)(2,1)S(1)}, bf16[3,72,2560]{2,1,0:T(8,128)(2,1)S(1)}, u32[]{:S(2)}, u32[]{:S(2)}) %collective-permute-start.21) | collective-permute-done | bytes 1105952 | tf_op jit(solution)/shard_map/ppermute | solution.py:30
  194.3 3.0 %collective-permute-start.22 = (bf16[72,2560]{1,0:T(8,128)(2,1)S(1)}, bf16[72,2560]{1,0:T(8,128)(2,1)S(1)}, u32[]{:S(2)}, u32[]{:S(2)}) collective-permute-start(bf16[72,2560]{1,0:T(8,128)(2,1)S(1)} %get-tuple-element.37), channel_id=1, source_target_pairs={{0,12},{1,13},{2,14},{3,15},{4,0},{5,1},{6,2},{7,3},{8,4},{9,5},{1... | collective-permute-start | bytes 1105928 | tf_op jit(solution)/shard_map/ppermute | solution.py:30
  197.3 2.3 %collective-permute-start.24 = (bf16[72,2560]{1,0:T(8,128)(2,1)S(1)}, bf16[72,2560]{1,0:T(8,128)(2,1)S(1)}, u32[]{:S(2)}, u32[]{:S(2)}) collective-permute-start(bf16[72,2560]{1,0:T(8,128)(2,1)S(1)} %get-tuple-element.35), channel_id=1, source_target_pairs={{0,8},{1,9},{2,10},{3,11},{4,12},{5,13},{6,14},{7,15},{8,0},{9,1},... | collective-permute-start | bytes 1105928 | tf_op jit(solution)/shard_map/ppermute | solution.py:30
  199.7 0.9 fusion.refs_0_
  200.6 5.8 %collective-permute-done.22.refs_1_ = bf16[72,2560]{1,0:T(8,128)(2,1)S(1)} collective-permute-done((bf16[72,2560]{1,0:T(8,128)(2,1)S(1)}, bf16[72,2560]{1,0:T(8,128)(2,1)S(1)}, u32[]{:S(2)}, u32[]{:S(2)}) %collective-permute-start.22) | collective-permute-done | bytes 368672 | tf_op jit(solution)/shard_map/ppermute | solution.py:30
  206.3 3.7 %collective-permute-done.23.refs_2_ = bf16[72,2560]{1,0:T(8,128)(2,1)S(1)} collective-permute-done((bf16[72,2560]{1,0:T(8,128)(2,1)S(1)}, bf16[72,2560]{1,0:T(8,128)(2,1)S(1)}, u32[]{:S(2)}, u32[]{:S(2)}) %collective-permute-start.23) | collective-permute-done | bytes 368672 | tf_op jit(solution)/shard_map/ppermute | solution.py:30
  210.0 0.7 copy-done.13
  210.9 4.1 %weigh_and_add.1 = bf16[128,2560]{1,0:T(8,128)(2,1)} custom-call(s32[1]{0:T(128)} %bitcast.y_ref, s32[128,2]{1,0:T(8,128)} %bitcast.34, s32[128,2]{1,0:T(8,128)} %bitcast.41, bf16[128,2560]{1,0:T(8,128)(2,1)} %bitcast.32, bf16[128,2560]{1,0:T(8,128)(2,1)} %get-tuple-element.20.normed_ref, f32[2,2560]{1,0:T(2,128)} %reshape.21.mod_ref, ...), custom_call_target="tpu_custom_call" | custom-call | flops 188743680 | bytes 3276800 | tf_op jit(solution)/shard_map/weigh_and_add/pallas_call | solution.py:287
  (88 shorter events, 2.8 us)
Async XLA Ops:
  0.0 71.9 %copy-start = (bf16[8,128,512]{2,1,0:T(8,128)(2,1)S(1)}, bf16[8,128,512]{2,1,0:T(8,128)(2,1)}, u32[]{:S(2)}) copy-start(bf16[8,128,512]{2,1,0:T(8,128)(2,1)} %param.11) | copy-start | bytes 3145732
  0.0 68.5 %collective-permute-start.4 = (bf16[1280,864]{0,1:T(8,128)(2,1)}, bf16[1280,864]{0,1:T(8,128)(2,1)}, u32[]{:S(2)}, u32[]{:S(2)}) collective-permute-start(bf16[1280,864]{0,1:T(8,128)(2,1)} %param.15), channel_id=1, source_target_pairs={{0,128},{128,0},{1,129},{129,1},{2,130},{130,2},{3,131},{131,3},{4... | collective-permute-start | bytes 6635528 | tf_op jit(solution)/shard_map/ppermute | solution.py:325
  0.0 71.8 %collective-permute-start.5 = (bf16[1280,864]{0,1:T(8,128)(2,1)}, bf16[1280,864]{0,1:T(8,128)(2,1)}, u32[]{:S(2)}, u32[]{:S(2)}) collective-permute-start(bf16[1280,864]{0,1:T(8,128)(2,1)} %param.16), channel_id=1, source_target_pairs={{0,128},{128,0},{1,129},{129,1},{2,130},{130,2},{3,131},{131,3},{4... | collective-permute-start | bytes 6635528 | tf_op jit(solution)/shard_map/ppermute | solution.py:325
  1.3 26.0 %copy-start.8 = (s32[1,128,2]{2,1,0:T(8,128)}, s32[1,128,2]{2,1,0:T(8,128)S(1)}, u32[]{:S(2)}) copy-start(s32[1,128,2]{2,1,0:T(8,128)S(1)} %copy.21) | copy-start | bytes 3076
  5.2 12.1 %collective-permute-start.11 = (bf16[72,2560]{1,0:T(8,128)(2,1)}, bf16[72,2560]{1,0:T(8,128)(2,1)S(1)}, u32[]{:S(2)}, u32[]{:S(2)}) collective-permute-start(bf16[72,2560]{1,0:T(8,128)(2,1)} %get-tuple-element.27), channel_id=1, source_target_pairs={{0,4},{1,5},{2,6},{3,7},{4,8},{5,9},{6,10},{7,11},{8,12},{9,13},{1... | collective-permute-start | bytes 1105928 | tf_op jit(solution)/shard_map/ppermute | solution.py:30
  6.7 11.7 %collective-permute-start.12 = (bf16[72,2560]{1,0:T(8,128)(2,1)}, bf16[72,2560]{1,0:T(8,128)(2,1)S(1)}, u32[]{:S(2)}, u32[]{:S(2)}) collective-permute-start(bf16[72,2560]{1,0:T(8,128)(2,1)} %get-tuple-element.28), channel_id=1, source_target_pairs={{0,12},{1,13},{2,14},{3,15},{4,0},{5,1},{6,2},{7,3},{8,4},{9,5},{1... | collective-permute-start | bytes 1105928 | tf_op jit(solution)/shard_map/ppermute | solution.py:30
  8.4 18.8 %collective-permute-start.13 = (bf16[72,2560]{1,0:T(8,128)(2,1)}, bf16[72,2560]{1,0:T(8,128)(2,1)S(1)}, u32[]{:S(2)}, u32[]{:S(2)}) collective-permute-start(bf16[72,2560]{1,0:T(8,128)(2,1)} %get-tuple-element.29), channel_id=1, source_target_pairs={{0,8},{1,9},{2,10},{3,11},{4,12},{5,13},{6,14},{7,15},{8,0},{9,1},... | collective-permute-start | bytes 1105928 | tf_op jit(solution)/shard_map/ppermute | solution.py:30
  17.2 93.8 %collective-permute-start.6 = (bf16[864,1280]{1,0:T(8,128)(2,1)}, bf16[864,1280]{1,0:T(8,128)(2,1)}, u32[]{:S(2)}, u32[]{:S(2)}) collective-permute-start(bf16[864,1280]{1,0:T(8,128)(2,1)} %down_own.3), channel_id=1, source_target_pairs={{0,128},{128,0},{1,129},{129,1},{2,130},{130,2},{3,131},{131,3},{4... | collective-permute-start | bytes 6635528 | tf_op jit(solution)/shard_map/ppermute | solution.py:325
  18.4 17.6 %collective-permute-start = (bf16[1,72,2560]{2,1,0:T(8,128)(2,1)}, bf16[1,72,2560]{2,1,0:T(8,128)(2,1)S(1)}, u32[]{:S(2)}, u32[]{:S(2)}) collective-permute-start(bf16[1,72,2560]{2,1,0:T(8,128)(2,1)} %bitcast.38), channel_id=1, source_target_pairs={{0,1},{1,2},{2,3},{3,0},{4,5},{5,6},{6,7},{7,4},{8,9},{9,10},{10,1... | collective-permute-start | bytes 1105928 | tf_op jit(solution)/shard_map/ppermute | solution.py:30
  27.2 12.4 %collective-permute-start.1 = (bf16[1,72,2560]{2,1,0:T(8,128)(2,1)}, bf16[1,72,2560]{2,1,0:T(8,128)(2,1)S(1)}, u32[]{:S(2)}, u32[]{:S(2)}) collective-permute-start(bf16[1,72,2560]{2,1,0:T(8,128)(2,1)} %bitcast.39), channel_id=1, source_target_pairs={{0,3},{1,0},{2,1},{3,2},{4,7},{5,4},{6,5},{7,6},{8,11},{9,8},{10,9... | collective-permute-start | bytes 1105928 | tf_op jit(solution)/shard_map/ppermute | solution.py:30
  27.2 12.4 %copy-start.22 = (s32[8]{0:T(128)S(1)}, s32[8]{0:T(128)}, u32[]{:S(2)}) copy-start(s32[8]{0:T(128)} %param.12) | copy-start | bytes 100
  27.3 41.2 %copy-start.2 = (bf16[3,72,2560]{2,1,0:T(8,128)(2,1)}, bf16[3,72,2560]{2,1,0:T(8,128)(2,1)S(1)}, u32[]{:S(2)}) copy-start(bf16[3,72,2560]{2,1,0:T(8,128)(2,1)S(1)} %pad_maximum_fusion.own_ref) | copy-start | bytes 3317764
  36.0 32.5 %copy-start.6 = (bf16[1,72,2560]{2,1,0:T(8,128)(2,1)}, bf16[1,72,2560]{2,1,0:T(8,128)(2,1)S(1)}, u32[]{:S(2)}) copy-start(bf16[1,72,2560]{2,1,0:T(8,128)(2,1)S(1)} %collective-permute-done.left_ref) | copy-start | bytes 1105924
  36.0 27.1 %collective-permute-start.14 = (bf16[3,72,2560]{2,1,0:T(8,128)(2,1)S(1)}, bf16[3,72,2560]{2,1,0:T(8,128)(2,1)S(1)}, u32[]{:S(2)}, u32[]{:S(2)}) collective-permute-start(bf16[3,72,2560]{2,1,0:T(8,128)(2,1)S(1)} %pad_maximum_fusion.own_ref), channel_id=1, source_target_pairs={{0,1},{1,2},{2,3},{3,0},{4,5},{5,6},{6,7},{7,4},{8,9},{9,10},{10,1... | collective-permute-start | bytes 3317768 | tf_op jit(solution)/shard_map/ppermute | solution.py:30
  39.6 28.9 %copy-start.7 = (bf16[1,72,2560]{2,1,0:T(8,128)(2,1)}, bf16[1,72,2560]{2,1,0:T(8,128)(2,1)S(1)}, u32[]{:S(2)}) copy-start(bf16[1,72,2560]{2,1,0:T(8,128)(2,1)S(1)} %collective-permute-done.1.right_ref) | copy-start | bytes 1105924
  39.6 28.1 %collective-permute-start.15 = (bf16[3,72,2560]{2,1,0:T(8,128)(2,1)S(1)}, bf16[3,72,2560]{2,1,0:T(8,128)(2,1)S(1)}, u32[]{:S(2)}, u32[]{:S(2)}) collective-permute-start(bf16[3,72,2560]{2,1,0:T(8,128)(2,1)S(1)} %pad_maximum_fusion.own_ref), channel_id=1, source_target_pairs={{0,3},{1,0},{2,1},{3,2},{4,7},{5,4},{6,5},{7,6},{8,11},{9,8},{10,9... | collective-permute-start | bytes 3317768 | tf_op jit(solution)/shard_map/ppermute | solution.py:30
  63.2 9.0 %copy-start.16 = (bf16[3,72,2560]{2,1,0:T(8,128)(2,1)}, bf16[3,72,2560]{2,1,0:T(8,128)(2,1)S(1)}, u32[]{:S(2)}) copy-start(bf16[3,72,2560]{2,1,0:T(8,128)(2,1)S(1)} %collective-permute-done.14.left_ref) | copy-start | bytes 3317764
  63.2 47.8 %collective-permute-start.2 = (bf16[1,72,1280]{2,1,0:T(8,128)(2,1)}, bf16[1,72,1280]{2,1,0:T(8,128)(2,1)S(1)}, u32[]{:S(2)}, u32[]{:S(2)}) collective-permute-start(bf16[1,72,1280]{2,1,0:T(8,128)(2,1)} %slice.60), channel_id=1, source_target_pairs={{0,1},{1,2},{2,3},{3,0},{4,5},{5,6},{6,7},{7,4},{8,9},{9,10},{10,1... | collective-permute-start | bytes 552968 | tf_op jit(solution)/shard_map/ppermute | solution.py:30
  66.8 5.3 %copy-start.15 = (bf16[512,320]{0,1:T(8,128)(2,1)S(1)}, bf16[512,320]{0,1:T(8,128)(2,1)}, u32[]{:S(2)}) copy-start(bf16[512,320]{0,1:T(8,128)(2,1)} %param.13) | copy-start | bytes 983044
  67.7 26.2 %copy-start.1 = (bf16[1280,864]{0,1:T(8,128)(2,1)S(1)}, bf16[1280,864]{0,1:T(8,128)(2,1)}, u32[]{:S(2)}) copy-start(bf16[1280,864]{0,1:T(8,128)(2,1)} %param.15) | copy-start | bytes 6635524
  67.7 4.6 %copy-start.17 = (bf16[3,72,2560]{2,1,0:T(8,128)(2,1)}, bf16[3,72,2560]{2,1,0:T(8,128)(2,1)S(1)}, u32[]{:S(2)}) copy-start(bf16[3,72,2560]{2,1,0:T(8,128)(2,1)S(1)} %collective-permute-done.15.right_ref) | copy-start | bytes 3317764
  67.7 43.3 %collective-permute-start.3 = (bf16[1,72,1280]{2,1,0:T(8,128)(2,1)}, bf16[1,72,1280]{2,1,0:T(8,128)(2,1)}, u32[]{:S(2)}, u32[]{:S(2)}) collective-permute-start(bf16[1,72,1280]{2,1,0:T(8,128)(2,1)} %slice.61), channel_id=1, source_target_pairs={{0,3},{1,0},{2,1},{3,2},{4,7},{5,4},{6,5},{7,6},{8,11},{9,8},{10,9... | collective-permute-start | bytes 552968 | tf_op jit(solution)/shard_map/ppermute | solution.py:30
  68.5 55.4 %collective-permute-start.16 = (bf16[3,72,1280]{2,1,0:T(8,128)(2,1)}, bf16[3,72,1280]{2,1,0:T(8,128)(2,1)}, u32[]{:S(2)}, u32[]{:S(2)}) collective-permute-start(bf16[3,72,1280]{2,1,0:T(8,128)(2,1)} %slice.62), channel_id=1, source_target_pairs={{0,1},{1,2},{2,3},{3,0},{4,5},{5,6},{6,7},{7,4},{8,9},{9,10},{10,1... | collective-permute-start | bytes 1658888 | tf_op jit(solution)/shard_map/ppermute | solution.py:30
  71.9 52.1 %collective-permute-start.17 = (bf16[3,72,1280]{2,1,0:T(8,128)(2,1)}, bf16[3,72,1280]{2,1,0:T(8,128)(2,1)}, u32[]{:S(2)}, u32[]{:S(2)}) collective-permute-start(bf16[3,72,1280]{2,1,0:T(8,128)(2,1)} %slice.63), channel_id=1, source_target_pairs={{0,3},{1,0},{2,1},{3,2},{4,7},{5,4},{6,5},{7,6},{8,11},{9,8},{10,9... | collective-permute-start | bytes 1658888 | tf_op jit(solution)/shard_map/ppermute | solution.py:30
  84.6 16.9 %all-to-all-start.1 = ((f32[16,1,320]{2,1,0:T(1,128)}), f32[16,1,320]{2,1,0:T(1,128)S(1)}, u32[]{:S(2)}, u32[]{:S(2)}) async-start(f32[16,1,320]{2,1,0:T(1,128)} %broadcast_in_dim.4), calls=%async_computation.1 | async-start | bytes 49152 | tf_op jit(solution)/shard_map/all_to_all | solution.py:335
  122.8 27.4 %copy-start.19 = (bf16[2560,4]{0,1:T(4,128)(2,1)S(1)}, bf16[2560,4]{0,1:T(4,128)(2,1)}, u32[]{:S(2)}) copy-start(bf16[2560,4]{0,1:T(4,128)(2,1)} %param.14) | copy-start | bytes 61444
  122.8 28.6 %copy-start.20 = (s32[1,128,2]{1,2,0:T(2,128)S(1)}, s32[1,128,2]{1,2,0:T(2,128)}, u32[]{:S(2)}) copy-start(s32[1,128,2]{1,2,0:T(2,128)} %param.19) | copy-start | bytes 3076
  122.8 32.0 %copy-start.21 = (bf16[1,72,1280]{2,1,0:T(8,128)(2,1)S(1)}, bf16[1,72,1280]{2,1,0:T(8,128)(2,1)}, u32[]{:S(2)}) copy-start(bf16[1,72,1280]{2,1,0:T(8,128)(2,1)} %get-tuple-element.26) | copy-start | bytes 552964
  122.8 33.2 %copy-start.10 = (bf16[1,72,2560]{2,1,0:T(8,128)(2,1)S(1)}, bf16[1,72,2560]{2,1,0:T(8,128)(2,1)}, u32[]{:S(2)}) copy-start(bf16[1,72,2560]{2,1,0:T(8,128)(2,1)} %get-tuple-element.23) | copy-start | bytes 1105924
  122.8 33.1 %collective-permute-start.7 = (bf16[1,72,1280]{2,1,0:T(8,128)(2,1)}, bf16[1,72,1280]{2,1,0:T(8,128)(2,1)S(1)}, u32[]{:S(2)}, u32[]{:S(2)}) collective-permute-start(bf16[1,72,1280]{2,1,0:T(8,128)(2,1)} %get-tuple-element.24), channel_id=1, source_target_pairs={{0,3},{1,0},{2,1},{3,2},{4,7},{5,4},{6,5},{7,6},{8,11},{9,8},{10,9... | collective-permute-start | bytes 552968 | tf_op jit(solution)/shard_map/ppermute | solution.py:30
  149.6 12.7 %copy-start.5 = (bf16[3,72,2560]{2,1,0:T(8,128)(2,1)S(1)}, bf16[3,72,2560]{2,1,0:T(8,128)(2,1)}, u32[]{:S(2)}) copy-start(bf16[3,72,2560]{2,1,0:T(8,128)(2,1)} %get-tuple-element.31) | copy-start | bytes 3317764
  149.6 12.7 %collective-permute-start.18 = (bf16[3,72,1280]{2,1,0:T(8,128)(2,1)}, bf16[3,72,1280]{2,1,0:T(8,128)(2,1)S(1)}, u32[]{:S(2)}, u32[]{:S(2)}) collective-permute-start(bf16[3,72,1280]{2,1,0:T(8,128)(2,1)} %get-tuple-element.32), channel_id=1, source_target_pairs={{0,3},{1,0},{2,1},{3,2},{4,7},{5,4},{6,5},{7,6},{8,11},{9,8},{10,9... | collective-permute-start | bytes 1658888 | tf_op jit(solution)/shard_map/ppermute | solution.py:30
  152.1 15.7 %collective-permute-start.20 = (bf16[3,72,1280]{2,1,0:T(8,128)(2,1)}, bf16[3,72,1280]{2,1,0:T(8,128)(2,1)S(1)}, u32[]{:S(2)}, u32[]{:S(2)}) collective-permute-start(bf16[3,72,1280]{2,1,0:T(8,128)(2,1)} %get-tuple-element.34), channel_id=1, source_target_pairs={{0,1},{1,2},{2,3},{3,0},{4,5},{5,6},{6,7},{7,4},{8,9},{9,10},{10,1... | collective-permute-start | bytes 1658888 | tf_op jit(solution)/shard_map/ppermute | solution.py:30
  154.8 17.0 %collective-permute-start.9 = (bf16[1,72,1280]{2,1,0:T(8,128)(2,1)S(1)}, bf16[1,72,1280]{2,1,0:T(8,128)(2,1)S(1)}, u32[]{:S(2)}, u32[]{:S(2)}) collective-permute-start(bf16[1,72,1280]{2,1,0:T(8,128)(2,1)S(1)} %copy-done.21), channel_id=1, source_target_pairs={{0,1},{1,2},{2,3},{3,0},{4,5},{5,6},{6,7},{7,4},{8,9},{9,10},{10,1... | collective-permute-start | bytes 552968 | tf_op jit(solution)/shard_map/ppermute | solution.py:30
  162.4 5.4 %copy-start.4 = (bf16[3,72,2560]{2,1,0:T(8,128)(2,1)S(1)}, bf16[3,72,2560]{2,1,0:T(8,128)(2,1)}, u32[]{:S(2)}) copy-start(bf16[3,72,2560]{2,1,0:T(8,128)(2,1)} %get-tuple-element.33) | copy-start | bytes 3317764
  162.5 26.1 %collective-permute-start.19 = (bf16[3,72,2560]{2,1,0:T(8,128)(2,1)S(1)}, bf16[3,72,2560]{2,1,0:T(8,128)(2,1)S(1)}, u32[]{:S(2)}, u32[]{:S(2)}) collective-permute-start(bf16[3,72,2560]{2,1,0:T(8,128)(2,1)S(1)} %pad_maximum_fusion.1), channel_id=1, source_target_pairs={{0,3},{1,0},{2,1},{3,2},{4,7},{5,4},{6,5},{7,6},{8,11},{9,8},{10,9... | collective-permute-start | bytes 3317768 | tf_op jit(solution)/shard_map/ppermute | solution.py:30
  167.9 3.9 %copy-start.9 = (bf16[1,72,2560]{2,1,0:T(8,128)(2,1)S(1)}, bf16[1,72,2560]{2,1,0:T(8,128)(2,1)}, u32[]{:S(2)}) copy-start(bf16[1,72,2560]{2,1,0:T(8,128)(2,1)} %get-tuple-element.25) | copy-start | bytes 1105924
  168.0 25.7 %collective-permute-start.21 = (bf16[3,72,2560]{2,1,0:T(8,128)(2,1)S(1)}, bf16[3,72,2560]{2,1,0:T(8,128)(2,1)S(1)}, u32[]{:S(2)}, u32[]{:S(2)}) collective-permute-start(bf16[3,72,2560]{2,1,0:T(8,128)(2,1)S(1)} %pad_maximum_fusion.2), channel_id=1, source_target_pairs={{0,1},{1,2},{2,3},{3,0},{4,5},{5,6},{6,7},{7,4},{8,9},{9,10},{10,1... | collective-permute-start | bytes 3317768 | tf_op jit(solution)/shard_map/ppermute | solution.py:30
  171.7 22.1 %copy-start.3 = (bf16[3,72,2560]{2,1,0:T(8,128)(2,1)S(1)}, bf16[3,72,2560]{2,1,0:T(8,128)(2,1)}, u32[]{:S(2)}) copy-start(bf16[3,72,2560]{2,1,0:T(8,128)(2,1)} %get-tuple-element.30) | copy-start | bytes 3317764
  171.7 28.0 %collective-permute-start.8 = (bf16[1,72,2560]{2,1,0:T(8,128)(2,1)S(1)}, bf16[1,72,2560]{2,1,0:T(8,128)(2,1)S(1)}, u32[]{:S(2)}, u32[]{:S(2)}) collective-permute-start(bf16[1,72,2560]{2,1,0:T(8,128)(2,1)S(1)} %pad_maximum_fusion.3), channel_id=1, source_target_pairs={{0,3},{1,0},{2,1},{3,2},{4,7},{5,4},{6,5},{7,6},{8,11},{9,8},{10,9... | collective-permute-start | bytes 1105928 | tf_op jit(solution)/shard_map/ppermute | solution.py:30
  171.9 27.8 %collective-permute-start.10 = (bf16[1,72,2560]{2,1,0:T(8,128)(2,1)S(1)}, bf16[1,72,2560]{2,1,0:T(8,128)(2,1)S(1)}, u32[]{:S(2)}, u32[]{:S(2)}) collective-permute-start(bf16[1,72,2560]{2,1,0:T(8,128)(2,1)S(1)} %pad_maximum_fusion.4), channel_id=1, source_target_pairs={{0,1},{1,2},{2,3},{3,0},{4,5},{5,6},{6,7},{7,4},{8,9},{9,10},{10,1... | collective-permute-start | bytes 1105928 | tf_op jit(solution)/shard_map/ppermute | solution.py:30
  194.2 5.4 %copy-start.11 = (bf16[1,72,2560]{2,1,0:T(8,128)(2,1)S(1)}, bf16[1,72,2560]{2,1,0:T(8,128)(2,1)}, u32[]{:S(2)}) copy-start(bf16[1,72,2560]{2,1,0:T(8,128)(2,1)} %get-tuple-element.22) | copy-start | bytes 1105924
  194.3 12.0 %collective-permute-start.22 = (bf16[72,2560]{1,0:T(8,128)(2,1)S(1)}, bf16[72,2560]{1,0:T(8,128)(2,1)S(1)}, u32[]{:S(2)}, u32[]{:S(2)}) collective-permute-start(bf16[72,2560]{1,0:T(8,128)(2,1)S(1)} %get-tuple-element.37), channel_id=1, source_target_pairs={{0,12},{1,13},{2,14},{3,15},{4,0},{5,1},{6,2},{7,3},{8,4},{9,5},{1... | collective-permute-start | bytes 1105928 | tf_op jit(solution)/shard_map/ppermute | solution.py:30
  197.3 12.7 %collective-permute-start.23 = (bf16[72,2560]{1,0:T(8,128)(2,1)S(1)}, bf16[72,2560]{1,0:T(8,128)(2,1)S(1)}, u32[]{:S(2)}, u32[]{:S(2)}) collective-permute-start(bf16[72,2560]{1,0:T(8,128)(2,1)S(1)} %get-tuple-element.36), channel_id=1, source_target_pairs={{0,4},{1,5},{2,6},{3,7},{4,8},{5,9},{6,10},{7,11},{8,12},{9,13},{1... | collective-permute-start | bytes 1105928 | tf_op jit(solution)/shard_map/ppermute | solution.py:30
  197.3 12.7 %collective-permute-start.24 = (bf16[72,2560]{1,0:T(8,128)(2,1)S(1)}, bf16[72,2560]{1,0:T(8,128)(2,1)S(1)}, u32[]{:S(2)}, u32[]{:S(2)}) collective-permute-start(bf16[72,2560]{1,0:T(8,128)(2,1)S(1)} %get-tuple-element.35), channel_id=1, source_target_pairs={{0,8},{1,9},{2,10},{3,11},{4,12},{5,13},{6,14},{7,15},{8,0},{9,1},... | collective-permute-start | bytes 1105928 | tf_op jit(solution)/shard_map/ppermute | solution.py:30
  206.3 3.7 %copy-start.12 = (bf16[72,2560]{1,0:T(8,128)(2,1)}, bf16[72,2560]{1,0:T(8,128)(2,1)S(1)}, u32[]{:S(2)}) copy-start(bf16[72,2560]{1,0:T(8,128)(2,1)S(1)} %collective-permute-done.22.refs_1_) | copy-start | bytes 1105924
  210.0 0.7 copy-start.13
  210.0 0.9 copy-start.14
  (1 other events, 0.7 us)
